TPU v7x, 32 devices: a whole 2x2x4 slice. The times are simulated.
32 devices in a mesh: groups: 2 (over y), blk: 4 (over z), term: 2 (over x), rep: 2 (over core).
Axes of the slice: x: 2, y: 2, z: 4, core: 2. Of those that a mesh axis runs over, the one named last changes fastest.
Arguments:
- wavefunction: bfloat16 [2048, 512], P(('groups', 'blk'), 'rep'), parts along dimension 0, may hold values from -6 to 6
- left_env: bfloat16 [2048, 16, 512], P(('groups', 'blk'), 'term'), parts along dimension 0, may hold values from -0.0625 to 0.0625
- right_env: bfloat16 [2048, 16, 512], P(('groups', 'blk'), 'term', 'rep'), parts along dimension 0, may hold values from -0.25 to 0.25
- sources: int32 [32, 2], P('groups'), parts along dimension 0, may hold values from 0 to 1
- live_dims: int32 [4, 2], P('groups'), parts along dimension 0, may hold values from 64 to 512, as said below
Outputs:
- next_basis: bfloat16 [2048, 512], P(('groups', 'blk', 'term', 'rep')), parts along dimension 0
- second_image: bfloat16 [2048, 512], P(('groups', 'blk', 'term', 'rep')), parts along dimension 0
- projection: float32 [4], P('groups'), parts along dimension 0
There are 2 independent parts, one for each index of `groups`. A program takes and returns all parts, laid end to end along the dimension named above; each array names one. Nothing has to cross between parts.
Inputs may be any that keep to these rules, and one draw needn't show every extreme that they name: `live_dims`: live rows and columns of each sector block; in some block both equal 512.
All inputs are finite; a program needn't handle non-finite values.
Results may differ from a plain program's by a relative error of at most 0.009.
Values may be sent and summed in bfloat16 or wider, within the bound.
A program may use at most 64 MiB of HBM per device.

v0:
```python
import jax
import jax.numpy as jnp
from jax import lax
from jax.sharding import PartitionSpec as P

M = 512
TERM_DEV = 8


EPSILON = 1e-06


def swapped(value, axis, bit):
    mask = 2**bit
    pairs = [(source, source ^ mask) for source in range(lax.axis_size(axis))]
    return lax.ppermute(value, axis, pairs)


def local(wavefunction, left_env, right_env, sources, live_dims):
    half_cols = wavefunction.shape[1]
    shard_rows = wavefunction.shape[0]
    term_count = lax.axis_size("term")
    rep_count = lax.axis_size("rep")
    blk_index = lax.axis_index("blk")
    term_index = lax.axis_index("term")
    rep_index = lax.axis_index("rep")
    blocks = live_dims.shape[0]
    own_block = blk_index // 2
    upper_half = blk_index % 2
    rows_out = shard_rows // (term_count * rep_count)
    row_slot = term_index * rep_count + rep_index
    env_other = swapped(right_env, "blk", 0)
    right_full = jnp.where(
        upper_half == 0,
        jnp.concatenate([right_env, env_other], 0),
        jnp.concatenate([env_other, right_env], 0),
    )
    all_sources = sources[:, own_block]
    my_sources = lax.dynamic_slice_in_dim(all_sources, term_index * TERM_DEV, TERM_DEV)
    source_rows = live_dims[my_sources, 0]
    source_cols = live_dims[my_sources, 1]
    row_ids = jnp.arange(M, dtype=jnp.int32)
    col_ids = rep_index * half_cols + jnp.arange(half_cols, dtype=jnp.int32)
    source_live = (row_ids[None, :, None] < source_rows[:, None, None]) & (
        col_ids[None, None, :] < source_cols[:, None, None]
    )
    out_rows = upper_half * shard_rows + row_slot * rows_out + jnp.arange(rows_out, dtype=jnp.int32)
    out_live = (out_rows[:, None] < live_dims[own_block, 0]) & (
        row_ids[None, :] < live_dims[own_block, 1]
    )

    def fetch_sources(local_block):
        all_blocks = lax.all_gather(local_block, "blk", axis=0, tiled=True)
        return all_blocks.reshape(blocks, M, half_cols)[my_sources]

    def apply_hamiltonian(local_block):
        fetched = jnp.where(source_live, fetch_sources(local_block), jnp.zeros((), jnp.bfloat16))
        halfway = jnp.einsum(
            "awc,wcb->wab", left_env, fetched, preferred_element_type=jnp.float32
        ).astype(jnp.bfloat16)
        partial_value = jnp.einsum(
            "wab,dwb->ad", halfway, right_full, preferred_element_type=jnp.float32
        )
        summed = lax.psum_scatter(partial_value, ("term", "rep"), scatter_dimension=0, tiled=True)
        return jnp.where(out_live, summed, jnp.zeros((), jnp.float32))

    sent_rows = lax.dynamic_slice_in_dim(
        wavefunction, (term_index * rep_count + (1 - rep_index)) * rows_out, rows_out, 0
    )
    received_rows = swapped(sent_rows, "rep", 0)
    kept_rows = lax.dynamic_slice_in_dim(wavefunction, row_slot * rows_out, rows_out, 0)
    assembled = jnp.where(
        rep_index == 0,
        jnp.concatenate([kept_rows, received_rows], 1),
        jnp.concatenate([received_rows, kept_rows], 1),
    )
    start_float = jnp.where(out_live, assembled, jnp.zeros((), jnp.bfloat16)).astype(jnp.float32)
    first_image = apply_hamiltonian(wavefunction)
    self_local = jnp.sum(start_float * start_float)
    cross_local = jnp.sum(start_float * first_image)
    self_product, cross_product = lax.psum((self_local, cross_local), ("blk", "term", "rep"))
    rayleigh = cross_product / (self_product + EPSILON)
    residual = first_image - rayleigh * start_float
    residual_square = lax.psum(jnp.sum(residual * residual), ("blk", "term", "rep"))
    entry_count = jnp.float32(blocks * M * M)
    norm_scale = lax.rsqrt(residual_square / entry_count + EPSILON)
    next_basis = (residual * norm_scale).astype(jnp.bfloat16)
    basis_half = lax.all_gather(next_basis, ("term", "rep"), axis=0, tiled=True)
    basis_local = lax.dynamic_slice_in_dim(basis_half, rep_index * half_cols, half_cols, 1)
    image_float = apply_hamiltonian(basis_local)
    image_correlation = lax.psum(
        jnp.sum(next_basis.astype(jnp.float32) * image_float), ("blk", "term", "rep")
    )
    projection = jnp.stack([rayleigh, image_correlation / entry_count])
    return (next_basis, image_float.astype(jnp.bfloat16), projection)


def solution(mesh):
    return jax.shard_map(
        local,
        mesh=mesh,
        in_specs=(
            P(("groups", "blk"), "rep"),
            P(("groups", "blk"), "term", None),
            P(("groups", "blk"), "term", "rep"),
            P("groups", None),
            P("groups", None),
        ),
        out_specs=(
            P(("groups", "blk", "term", "rep"), None),
            P(("groups", "blk", "term", "rep"), None),
            P("groups"),
        ),
        check_vma=False,
    )
```

profile of v0, /device:TPU:0, one launch (start us, length us, event | category | flops | bytes accessed | tf_op | source)
XLA Modules:
  0.0 241.6 jit_solution(890763630197925050)
XLA Ops:
  7.2 0.0 reduce-scatter.3.cloned.1.call-start
  7.2 3.1 %collective-permute-start = (bf16[256,8,256]{2,1,0:T(8,128)(2,1)}, bf16[256,8,256]{2,1,0:T(8,128)(2,1)}, u32[]{:S(2)}, u32[]{:S(2)}) collective-permute-start(bf16[256,8,256]{2,1,0:T(8,128)(2,1)} %param.7), channel_id=1, source_target_pairs={{0,4},{4,0},{8,12},{12,8},{1,5},{5,1},{9,13},{13,9},{2,6},{6,2},{1... | collective-permute-start | bytes 3145736 | tf_op jit(solution)/shard_map/ppermute | solution.py:16
  10.3 0.8 fusion.26
  11.1 1.3 gather_fusion.1
  12.4 1.3 gather_fusion
  13.7 0.0 copy-start.2
  13.7 3.0 %copy.12 = bf16[256,8,512]{0,2,1:T(8,128)(2,1)S(1)} copy(bf16[256,8,512]{2,1,0:T(8,128)(2,1)} %param.6) | data formatting | bytes 4194304 | tf_op args[1]
  16.8 0.0 copy-done.2
  16.8 30.2 %all_gather.9 = bf16[1024,256]{1,0:T(8,128)(2,1)S(1)} all-gather(bf16[256,256]{1,0:T(8,128)(2,1)S(1)} %copy-done.2), channel_id=1, replica_groups=mesh['groups'=2,'blk'=4,'term'=2,'rep'=2] {'blk'}, dimensions={0}, use_global_device_ids=true | all-gather | bytes 655360 | tf_op jit(solution)/shard_map/all_gather | solution.py:53
  47.0 2.0 gather_fusion.2
  48.9 0.1 broadcast_compare_fusion
  49.0 0.1 iota_compare_fusion
  49.1 0.0 collective-permute-done
  49.1 3.9 %maximum_select_fusion = bf16[512,8,256]{2,1,0:T(8,128)(2,1)} fusion(bf16[256,8,256]{2,1,0:T(8,128)(2,1)} %collective-permute-done, bf16[256,8,256]{2,1,0:T(8,128)(2,1)} %param.7, pred[]{:T(512)S(6)} %eq.8), kind=kLoop, calls=%fused_computation.8 | loop fusion | flops 3145728 | bytes 4194305 | tf_op jit(solution)/shard_map/jit(_where)/select_n | solution.py:33
  53.0 0.0 copy-start
  53.0 5.0 %fusion.14 = f32[256,512]{1,0:T(8,128)} fusion(bf16[512,8,256]{2,1,0:T(8,128)(2,1)} %maximum_select_fusion, bf16[256,8,512]{0,2,1:T(8,128)(2,1)S(1)} %copy.12, bf16[8,512,256]{2,1,0:T(8,128)(2,1)} %gather_fusion.2, pred[8,256]{1,0:T(8,128)(4,1)S(1)} %broadcast_compare_fusion, pred[8,512]{1,0:T(8,128)(4,1)S(1)} %iota_compare_fusion), kind=kOutput, calls=%fused_computation.21 | convolution fusion | flops 1076363264 | bytes 6821888 | tf_op jit(solution)/shard_map/wab,dwb->ad/dot_general | solution.py:61
  58.1 0.0 reduce-scatter.3.cloned.1.call-update
  58.1 0.0 reduce-scatter.5.cloned.1.call-start
  58.2 0.1 collective-permute-start.1
  58.2 0.0 copy-done
  58.3 0.6 constant_dynamic-slice_fusion.3
  58.8 0.6 iota_compare_fusion.1
  59.5 0.7 add_compare_fusion
  60.2 0.0 collective-permute-done.1
  60.2 19.9 %reduce-scatter.3.cloned.1.call-done = f32[64,512]{1,0:T(8,128)} async-done(((f32[256,512]{1,0:T(8,128)}), f32[64,512]{1,0:T(8,128)}) %reduce-scatter.3.cloned.1.call-update) | async-done | bytes 131088 | tf_op jit(solution)/shard_map/reduce_scatter | solution.py:64
  80.0 1.6 fusion.23
  81.7 32.9 %all-reduce.2 = (f32[]{:T(128)}, f32[]{:T(128)}) all-reduce(f32[]{:T(128)} %get-tuple-element.4, f32[]{:T(128)} %get-tuple-element.3), channel_id=1, replica_groups=mesh['groups'=2,'blk'=4,'term'=2,'rep'=2] {'blk','term','rep'}, use_global_device_ids=true, to_apply=%region_2.3 | all-reduce | flops 2 | bytes 16 | tf_op jit(solution)/shard_map/psum | solution.py:81
  115.8 1.6 multiply_reduce_fusion.1
  117.5 30.1 %psum.30 = f32[]{:T(128)} all-reduce(f32[]{:T(128)} %multiply_reduce_fusion.1), channel_id=1, replica_groups=mesh['groups'=2,'blk'=4,'term'=2,'rep'=2] {'blk','term','rep'}, use_global_device_ids=true, to_apply=%region_6.7 | all-reduce | flops 1 | bytes 8 | tf_op jit(solution)/shard_map/psum | solution.py:84
  148.3 1.0 multiply_convert_fusion
  149.3 0.0 copy-start.1
  149.3 5.8 %all_gather.10 = bf16[256,512]{1,0:T(8,128)(2,1)S(1)} all-gather(bf16[64,512]{1,0:T(8,128)(2,1)S(1)} %multiply_convert_fusion), channel_id=1, replica_groups=mesh['groups'=2,'blk'=4,'term'=2,'rep'=2] {'term','rep'}, dimensions={0}, use_global_device_ids=true | all-gather | bytes 327680 | tf_op jit(solution)/shard_map/all_gather | solution.py:88
  155.1 16.1 %all_gather.11 = bf16[1024,256]{1,0:T(8,128)(2,1)S(1)} all-gather(bf16[256,256]{1,0:T(8,128)(2,1)S(1)} %constant_dynamic-slice_fusion.2), channel_id=1, replica_groups=mesh['groups'=2,'blk'=4,'term'=2,'rep'=2] {'blk'}, dimensions={0}, use_global_device_ids=true | all-gather | bytes 655360 | tf_op jit(solution)/shard_map/all_gather | solution.py:53
  171.2 2.0 gather_fusion.3
  173.2 5.0 %fusion.17 = f32[256,512]{1,0:T(8,128)} fusion(bf16[512,8,256]{2,1,0:T(8,128)(2,1)} %maximum_select_fusion, bf16[256,8,512]{0,2,1:T(8,128)(2,1)S(1)} %copy.12, bf16[8,512,256]{2,1,0:T(8,128)(2,1)} %gather_fusion.3, pred[8,256]{1,0:T(8,128)(4,1)S(1)} %broadcast_compare_fusion, pred[8,512]{1,0:T(8,128)(4,1)S(1)} %iota_compare_fusion), kind=kOutput, calls=%fused_computation.22 | convolution fusion | flops 1076363264 | bytes 6821888 | tf_op jit(solution)/shard_map/wab,dwb->ad/dot_general | solution.py:61
  178.2 0.0 reduce-scatter.5.cloned.1.call-update
  178.2 19.2 %reduce-scatter.5.cloned.1.call-done = f32[64,512]{1,0:T(8,128)} async-done(((f32[256,512]{1,0:T(8,128)}), f32[64,512]{1,0:T(8,128)}) %reduce-scatter.5.cloned.1.call-update) | async-done | bytes 131088 | tf_op jit(solution)/shard_map/reduce_scatter | solution.py:64
  197.4 0.0 copy-done.1
  197.4 1.6 multiply_reduce_fusion
  199.0 32.9 %psum.31 = f32[]{:T(128)} all-reduce(f32[]{:T(128)} %multiply_reduce_fusion), channel_id=1, replica_groups=mesh['groups'=2,'blk'=4,'term'=2,'rep'=2] {'blk','term','rep'}, use_global_device_ids=true, to_apply=%region_9.10 | all-reduce | flops 1 | bytes 8 | tf_op jit(solution)/shard_map/psum | solution.py:91
  232.5 0.6 pad_maximum_fusion
  233.1 1.6 fusion.25
  (5 shorter events, 0.0 us)
Async XLA Ops:
  7.2 72.9 %reduce-scatter.3.cloned.1.call-start = ((), (), s32[]{:S(2)}) async-start(), calls=%async_computation.2 | async-start | bytes 655360 | tf_op jit(solution)/shard_map/reduce_scatter | solution.py:64
  7.2 41.9 %collective-permute-start = (bf16[256,8,256]{2,1,0:T(8,128)(2,1)}, bf16[256,8,256]{2,1,0:T(8,128)(2,1)}, u32[]{:S(2)}, u32[]{:S(2)}) collective-permute-start(bf16[256,8,256]{2,1,0:T(8,128)(2,1)} %param.7), channel_id=1, source_target_pairs={{0,4},{4,0},{8,12},{12,8},{1,5},{5,1},{9,13},{13,9},{2,6},{6,2},{1... | collective-permute-start | bytes 3145736 | tf_op jit(solution)/shard_map/ppermute | solution.py:16
  13.7 3.1 %copy-start.2 = (bf16[256,256]{1,0:T(8,128)(2,1)S(1)}, bf16[256,256]{1,0:T(8,128)(2,1)}, u32[]{:S(2)}) copy-start(bf16[256,256]{1,0:T(8,128)(2,1)} %param.5) | copy-start | bytes 393220
  53.0 5.2 %copy-start = (s32[2,2]{1,0:T(2,128)S(1)}, s32[2,2]{1,0:T(2,128)}, u32[]{:S(2)}) copy-start(s32[2,2]{1,0:T(2,128)} %param.9) | copy-start | bytes 52
  58.1 139.3 %reduce-scatter.5.cloned.1.call-start = ((), (), s32[]{:S(2)}) async-start(), calls=%async_computation.3 | async-start | bytes 655360 | tf_op jit(solution)/shard_map/reduce_scatter | solution.py:64
  58.2 2.0 collective-permute-start.1
  149.3 48.1 %copy-start.1 = (bf16[64,512]{1,0:T(8,128)(2,1)}, bf16[64,512]{1,0:T(8,128)(2,1)S(1)}, u32[]{:S(2)}) copy-start(bf16[64,512]{1,0:T(8,128)(2,1)S(1)} %multiply_convert_fusion) | copy-start | bytes 196612
Sparse Core Ops, SparseCore 0:
  58.2 21.8 reduce-scatter.2
  178.3 19.0 reduce-scatter.4
where the time goes:
time: 242 us
  blocking collectives  148 us (61%)
  waiting for transfers between devices  39.1 us (16%)
  between operations  16.8 us (7%)
  other arithmetic  14.2 us (6%)
  local copies, waits for them, and re-layouts  10.3 us (4%)
  matrix products  10.1 us (4%)
  starting transfers between devices  3.24 us (1%)
    all_gather x2, blocking collectives, fetch_sources(): all_blocks = lax.all_gather(local_block, 'blk', axis=0, tiled=True)  46.2 us
    reduce_scatter x2, waiting for transfers between devices, apply_hamiltonian(): lax.psum_scatter(partial_value, ('term', 'rep'), scatter_dimension=0, til...  39.1 us
    psum x1, blocking collectives, local(): lax.psum((self_local, cross_local), ('blk', 'term', 'rep'))  32.9 us
    psum x1, blocking collectives, local(): lax.psum(jnp.sum(next_basis.astype(jnp.float32) * image_float), ('blk', '...  32.9 us
    psum x1, blocking collectives, local(): lax.psum(jnp.sum(residual * residual), ('blk', 'term', 'rep'))  30.1 us
    dot_general x2, matrix products, apply_hamiltonian(): jnp.einsum('wab,dwb->ad', halfway, right_full, preferred_element_type=jnp...  10.1 us
    all_gather x1, blocking collectives, local(): basis_half = lax.all_gather(next_basis, ('term', 'rep'), axis=0, tiled=True)  5.79 us
  transfers between devices with their start and end apart: 4, of which 2 were waited for; matrix products, arithmetic and copies ran while one was open for 4% of the time, Pallas kernels for 0%

commit v1 on v0

v1 whole, which is shorter than its diff:
```python
import functools

import jax
import jax.numpy as jnp
from jax import lax
from jax.experimental import pallas as pl
from jax.experimental.pallas import tpu as pltpu
from jax.sharding import PartitionSpec as P

EPSILON = 1e-06
MESH = pl.DeviceIdType.MESH
F32 = jnp.float32
BF16 = jnp.bfloat16


def kernel(
    B, T, R, blocks,
    wf, left, right, sources, live,
    nb_out, img_out, proj_out,
    left_raw, left_f, left_w, right_raw, right_got, right_f, right_w,
    v1, vm, v2, sbuf, half, part1, part2, red1, red2, f_ref, fb, sc_a, sc_b, sc_c, sc_d,
    loc_sem, rsend, rrecv, v_send, v_recv, vx_send, vx_recv, s_sem,
    p1_send, p1_recv, p2_send, p2_recv, g_send, g_recv, gx_send, gx_recv,
    sc_send, sc_recv,
):
    TR = T * R
    b, t, r = lax.axis_index("blk"), lax.axis_index("term"), lax.axis_index("rep")
    slot = t * R + r
    rows, W, M = left.shape
    ro = rows // TR
    hc = M // R
    qc = M // 4
    own, u = b // 2, b % 2

    def copy(src, dst, ss, rs, bb, tt, rr):
        return pltpu.make_async_remote_copy(
            src_ref=src, dst_ref=dst, send_sem=ss, recv_sem=rs,
            device_id={"blk": bb, "term": tt, "rep": rr}, device_id_type=MESH)

    def zpeer(k):
        return lax.rem(b + k, B)

    def zfrom(k):
        return lax.rem(b - k + B, B)

    def speer(k):
        p = lax.rem(slot + k, TR)
        return p // R, lax.rem(p, R)

    barrier = pltpu.get_barrier_semaphore()
    for k in range(B):
        for j in range(R):
            if k or j:
                pl.semaphore_signal(barrier, inc=1, device_id={"blk": zpeer(k), "term": t, "rep": lax.rem(r + j, R)}, device_id_type=MESH)
    for k in range(1, TR):
        tt, rr = speer(k)
        pl.semaphore_signal(barrier, inc=1, device_id={"blk": b, "term": tt, "rep": rr}, device_id_type=MESH)

    lcopy = pltpu.make_async_copy(left, left_raw, loc_sem.at[0])
    lcopy.start()
    rcopy = pltpu.make_async_copy(right, right_raw, loc_sem.at[1])
    rcopy.start()
    pl.semaphore_wait(barrier, B * R - 1 + TR - 1)

    def piece(buf, bb, start, n):
        return buf.at[bb // 2, pl.ds((bb % 2) * TR + start, n)]

    vz = []
    for k in range(1, B):
        c = copy(wf.at[pl.ds(t * R, R)], piece(v1, b, t * R, R), v_send.at[k - 1], v_recv.at[k - 1], zpeer(k), t, r)
        c.start()
        vz.append(c)
    mine = [copy(wf.at[t * R + lax.rem(r + 1, R)], sbuf, s_sem.at[0], s_sem.at[1], b, t, lax.rem(r + 1, R))]
    mine[0].start()
    other = b + 1 - 2 * u
    chunk = rows // 2
    rz = []
    for c in range(2):
        d = pl.ds(c * chunk, chunk)
        cp = copy(right.at[d], right_got.at[d], rsend.at[c], rrecv.at[c], other, t, r)
        cp.start()
        rz.append(cp)

    v1[own, pl.ds(u * TR, TR)] = wf[...]

    lcopy.wait()
    left_f[...] = left_raw[...].astype(F32)
    for w in range(W):
        left_w[w] = left_f[:, w, :].astype(BF16)
    rcopy.wait()
    right_f[...] = right_raw[...].astype(F32)
    for w in range(W):
        right_w[u, :, w * hc:(w + 1) * hc] = right_f[:, w, :].astype(BF16)

    vx = []
    for k in range(1, B):
        src = zfrom(k)
        here = piece(v1, src, t * R, R)
        copy(here, here, v_send.at[k - 1], v_recv.at[k - 1], src, t, r).wait_recv()
        for j in range(1, T):
            c = copy(here, here, vx_send.at[k - 1, j - 1], vx_recv.at[k - 1, j - 1], b, lax.rem(t + j, T), r)
            c.start()
            vx.append(c)
    for k in range(1, B):
        src = zfrom(k)
        for j in range(1, T):
            tt = lax.rem(t - j + T, T)
            there = piece(v1, src, tt * R, R)
            copy(there, there, vx_send.at[k - 1, j - 1], vx_recv.at[k - 1, j - 1], b, tt, r).wait_recv()
    row_of = lax.broadcasted_iota(jnp.int32, (2 * TR, ro, hc), 0) * ro + lax.broadcasted_iota(jnp.int32, (2 * TR, ro, hc), 1)
    col_of = lax.broadcasted_iota(jnp.int32, (2 * TR, ro, hc), 2) + r * hc

    @pl.loop(0, blocks)
    def _(k):
        ok = (row_of < live[k, 0]) & (col_of < live[k, 1])
        vm[k] = jnp.where(ok, v1[k].astype(F32), 0.0).astype(BF16)

    def halfway(v):
        for w in range(W):
            src = sources[t * W + w, own]
            x = v[src].reshape(M, hc)
            half[:, w * hc:(w + 1) * hc] = jnp.dot(left_w[w], x, preferred_element_type=F32).astype(BF16)

    def product(h, lo, n):
        return lax.dot_general(half[...], right_w[h, lo:lo + n, :], (((1,), (1,)), ((), ())), preferred_element_type=F32)

    def scatter(part, red, sends, recvs, q, p):
        out = []
        for k in range(1, TR):
            tt, rr = speer(k)
            c = copy(part.at[q, pl.ds(lax.rem(slot + k, TR) * ro, ro)], red.at[q, k - 1],
                     sends.at[p, k - 1], recvs.at[p, k - 1], b, tt, rr)
            c.start()
            out.append(c)
        return out

    out_row = lax.broadcasted_iota(jnp.int32, (ro, M), 0) + u * rows + slot * ro
    out_col = lax.broadcasted_iota(jnp.int32, (ro, M), 1)
    out_live = (out_row < live[own, 0]) & (out_col < live[own, 1])

    def gathered(part, red):
        got = []
        for q in range(4):
            x = part[q, pl.ds(slot * ro, ro), :]
            for k in range(1, TR):
                x = x + red[q, k - 1]
            got.append(x)
        return jnp.where(out_live, jnp.concatenate(got, axis=1), 0.0)

    def await_all(copies):
        for c in copies:
            c.wait()

    halfway(vm)
    x = product(u, 0, 2 * qc)
    part1[2 * u] = x[:, :qc]
    part1[2 * u + 1] = x[:, qc:]
    p1 = scatter(part1, red1, p1_send, p1_recv, 2 * u, 0)
    p1 += scatter(part1, red1, p1_send, p1_recv, 2 * u + 1, 1)
    for c in range(2):
        rz[c].wait()
        lo = c * chunk
        right_f[lo:lo + chunk] = right_got[lo:lo + chunk].astype(F32)
        for w in range(W):
            right_w[1 - u, lo:lo + chunk, w * hc:(w + 1) * hc] = right_f[lo:lo + chunk, w, :].astype(BF16)
        part1[2 * (1 - u) + c] = product(1 - u, lo, chunk)
        p1 += scatter(part1, red1, p1_send, p1_recv, 2 * (1 - u) + c, 2 + c)

    mine[0].wait()
    kept = wf[slot]
    for_r0 = jnp.concatenate([kept, sbuf[...]], axis=1).astype(F32)
    for_r1 = jnp.concatenate([sbuf[...], kept], axis=1).astype(F32)
    start = jnp.where(out_live, jnp.where(r == 0, for_r0, for_r1), 0.0)
    await_all(p1)
    first = gathered(part1, red1)
    f_ref[...] = first

    for j in range(R):
        fb[j] = first[:, j * hc:(j + 1) * hc].astype(BF16)
    v2[own, u * TR + slot] = fb[r]
    gz = []
    for j in range(R):
        rr = lax.rem(r + j, R)
        for k in range(B):
            if k or j:
                i = j * B + k - 1
                c = copy(fb.at[rr], v2.at[own, u * TR + slot], g_send.at[i], g_recv.at[i], zpeer(k), t, rr)
                c.start()
                gz.append(c)

    def tile(*values):
        row = lax.broadcasted_iota(jnp.int32, (8, 128), 0)
        x = jnp.zeros((8, 128), F32)
        for i, value in enumerate(values):
            x = jnp.where(row == i, value, x)
        return x

    def spread(buf, index, base, n, to):
        out = []
        for k in range(1, n):
            c = copy(buf.at[index], buf.at[index], sc_send.at[base, k - 1], sc_recv.at[base, k - 1], *to(k))
            c.start()
            out.append(c)
        return out

    def to_slot(k):
        tt, rr = speer(k)
        return b, tt, rr

    def to_blk(k):
        return zpeer(k), t, r

    sc_a[slot] = tile(jnp.sum(start * start), jnp.sum(start * first), jnp.sum(first * first))
    s1 = spread(sc_a, slot, 0, TR, to_slot)

    gx = []
    for k in range(B):
        src = zfrom(k)
        for j in range(R):
            if k or j:
                i = j * B + k - 1
                rr = lax.rem(r - j + R, R)
                there = v2.at[src // 2, (src % 2) * TR + t * R + rr]
                copy(there, there, g_send.at[i], g_recv.at[i], src, t, rr).wait_recv()
        here = piece(v2, src, t * R, R)
        for j in range(1, T):
            c = copy(here, here, gx_send.at[k, j - 1], gx_recv.at[k, j - 1], b, lax.rem(t + j, T), r)
            c.start()
            gx.append(c)
    await_all(s1)
    total = sc_a[0]
    for i in range(1, TR):
        total = total + sc_a[i]
    sc_b[b] = total
    s2 = spread(sc_b, b, 1, B, to_blk)
    for k in range(B):
        src = zfrom(k)
        for j in range(1, T):
            tt = lax.rem(t - j + T, T)
            there = piece(v2, src, tt * R, R)
            copy(there, there, gx_send.at[k, j - 1], gx_recv.at[k, j - 1], b, tt, r).wait_recv()

    halfway(v2)
    p2 = []
    for i in range(2):
        h = u if i == 0 else 1 - u
        x = product(h, 0, 2 * qc)
        for c in range(2):
            part2[2 * h + c] = x[:, c * qc:(c + 1) * qc]
            p2 += scatter(part2, red2, p2_send, p2_recv, 2 * h + c, 2 * i + c)

    await_all(s2)
    total = sc_b[0]
    for i in range(1, B):
        total = total + sc_b[i]

    def row_value(x, i):
        return x[i:i + 1, 0:1]

    self_product, cross, square = row_value(total, 0), row_value(total, 1), row_value(total, 2)
    rayleigh = cross / (self_product + EPSILON)
    residual_square = jnp.maximum(square - 2.0 * rayleigh * cross + rayleigh * rayleigh * self_product, 0.0)
    entries = float(blocks * M * M)
    scale = lax.rsqrt(residual_square / entries + EPSILON)
    first = f_ref[...]
    nb = ((first - rayleigh * start) * scale).astype(BF16)
    nb_out[...] = nb

    await_all(p2)
    second = gathered(part2, red2)
    image = (second - rayleigh * f_ref[...]) * scale
    img_out[...] = image.astype(BF16)
    sc_c[slot] = tile(jnp.sum(nb.astype(F32) * image))
    await_all(spread(sc_c, slot, 2, TR, to_slot))
    total = sc_c[0]
    for i in range(1, TR):
        total = total + sc_c[i]
    sc_d[b] = total
    await_all(spread(sc_d, b, 3, B, to_blk))
    total = sc_d[0]
    for i in range(1, B):
        total = total + sc_d[i]
    lane = lax.broadcasted_iota(jnp.int32, (8, 128), 1)
    proj_out[...] = jnp.where(lane == 0, rayleigh, row_value(total, 0) / entries)
    for c in vz + vx + gz + gx:
        c.wait_send()


def local(wavefunction, left_env, right_env, sources, live_dims):
    B, T, R = lax.axis_size("blk"), lax.axis_size("term"), lax.axis_size("rep")
    TR = T * R
    rows, W, M = left_env.shape
    hc = M // R
    ro = rows // TR
    qc = M // 4
    blocks = live_dims.shape[0]
    vmem = pl.BlockSpec(memory_space=pltpu.VMEM)
    smem = pl.BlockSpec(memory_space=pltpu.SMEM)
    anyw = pl.BlockSpec(memory_space=pl.ANY)
    dma = pltpu.SemaphoreType.DMA
    V = pltpu.VMEM
    nb, img, proj = pl.pallas_call(
        functools.partial(kernel, B, T, R, blocks),
        out_shape=(
            jax.ShapeDtypeStruct((ro, M), BF16),
            jax.ShapeDtypeStruct((ro, M), BF16),
            jax.ShapeDtypeStruct((8, 128), F32),
        ),
        in_specs=[vmem, anyw, anyw, smem, smem],
        out_specs=(vmem, vmem, vmem),
        scratch_shapes=[
            V((rows, W, M), BF16), V((rows, W, M), F32), V((W, rows, M), BF16),
            V((rows, W, hc), BF16), V((rows, W, hc), BF16), V((rows, W, hc), F32),
            V((2, rows, W * hc), BF16),
            V((blocks, 2 * TR, ro, hc), BF16), V((blocks, 2 * TR, ro, hc), BF16), V((blocks, 2 * TR, ro, hc), BF16),
            V((ro, hc), BF16), V((rows, W * hc), BF16),
            V((4, rows, qc), F32), V((4, rows, qc), F32),
            V((4, TR - 1, ro, qc), F32), V((4, TR - 1, ro, qc), F32),
            V((ro, M), F32), V((R, ro, hc), BF16),
            V((TR, 8, 128), F32), V((B, 8, 128), F32), V((TR, 8, 128), F32), V((B, 8, 128), F32),
            dma((2,)), dma((2,)), dma((2,)), dma((B - 1,)), dma((B - 1,)), dma((B - 1, T - 1)), dma((B - 1, T - 1)), dma((2,)),
            dma((4, TR - 1)), dma((4, TR - 1)), dma((4, TR - 1)), dma((4, TR - 1)),
            dma((R * B - 1,)), dma((R * B - 1,)), dma((B, T - 1)), dma((B, T - 1)),
            dma((4, max(TR, B) - 1)), dma((4, max(TR, B) - 1)),
        ],
        compiler_params=pltpu.CompilerParams(collective_id=0, has_side_effects=True, vmem_limit_bytes=50 * 2**20),
    )(wavefunction.reshape(TR, ro, hc), left_env, right_env, sources, live_dims)
    return nb, img, proj[0, :2]


def solution(mesh):
    return jax.shard_map(
        local,
        mesh=mesh,
        in_specs=(
            P(("groups", "blk"), "rep"),
            P(("groups", "blk"), "term", None),
            P(("groups", "blk"), "term", "rep"),
            P("groups", None),
            P("groups", None),
        ),
        out_specs=(
            P(("groups", "blk", "term", "rep"), None),
            P(("groups", "blk", "term", "rep"), None),
            P("groups"),
        ),
        check_vma=False,
    )
```

time: 242 us -> 74.9 us (0.31)
  blocking collectives: 148 us -> 0 us
  Pallas kernels: 0 us -> 67.1 us
  waiting for transfers between devices: 39.1 us -> 0 us
  between operations: 16.8 us -> 0.64 us
  other arithmetic: 14.2 us -> 0 us
  matrix products: 10.1 us -> 0 us
  local copies, waits for them, and re-layouts: 10.3 us -> 6.92 us
  starting transfers between devices: 3.24 us -> 0 us
    psum x3 -> x0, blocking collectives: 95.8 us -> none  [the longest x1 32.9 us: local(): lax.psum((self_local, cross_local), ('blk', 'term', 'rep'))]
    pallas_call x0 -> x1, Pallas kernels: none -> 67.1 us  [local(): pl.pallas_call(functools.partial(kernel, B, T, R, blocks), out_shape=(jax...]
    all_gather x3 -> x0, blocking collectives: 52 us -> none  [the longest x2 46.2 us: fetch_sources(): all_blocks = lax.all_gather(local_block, 'blk', axis=0, tiled=True)]
    reduce_scatter x2 -> x0, waiting for transfers between devices: 39.1 us -> none  [apply_hamiltonian(): lax.psum_scatter(partial_value, ('term', 'rep'), scatter_dimension=0, til...]
    dot_general x2 -> x0, matrix products: 10.1 us -> none  [apply_hamiltonian(): jnp.einsum('wab,dwb->ad', halfway, right_full, preferred_element_type=jnp...]
    gather x4 -> x0, local copies, waits for them, and re-layouts: 6.61 us -> none  [the longest x2 3.95 us: fetch_sources(): return all_blocks.reshape(blocks, M, half_cols)[my_sources]]
    reduce_sum x3 -> x0, other arithmetic: 4.87 us -> none  [the longest x1 1.63 us: local(): jnp.sum(residual * residual)]
    select_n x1 -> x0, other arithmetic: 3.92 us -> none  [local(): jnp.where(upper_half == 0, jnp.concatenate([right_env, env_other], 0), jn...]
  transfers between devices with their start and end apart: 4 -> 0, of which waited for: 2 -> 0; matrix products, arithmetic and copies ran while one was open for 4% -> 0% of each run, Pallas kernels for 0% -> 0%
where the time goes in v1:
time: 74.9 us; the launch traced here: 74.7 us
  Pallas kernels  67.1 us (90%)
  local copies, waits for them, and re-layouts  6.92 us (9%)
    pallas_call x1, Pallas kernels, local(): pl.pallas_call(functools.partial(kernel, B, T, R, blocks), out_shape=(jax...  67.1 us
    unnamed x11, local copies, waits for them, and re-layouts  6.41 us

profile of v1, /device:TPU:0, one launch (start us, length us, event | category | flops | bytes accessed | tf_op | source)
XLA Modules:
  0.0 74.7 jit_solution(8723171069437195009)
XLA Ops:
  0.6 0.8 %copy.8.sources = s32[16,2]{1,0:T(8,128)S(1)} copy(s32[16,2]{0,1:T(2,128)} %param.8) | data formatting | bytes 256 | tf_op args[3]
  1.4 0.0 copy-start
  1.4 1.6 %copy-done = bf16[256,8,512]{2,1,0:T(8,128)(2,1)S(1)} copy-done((bf16[256,8,512]{2,1,0:T(8,128)(2,1)S(1)}, bf16[256,8,512]{2,1,0:T(8,128)(2,1)}, u32[]{:S(2)}) %copy-start) | copy-done | bytes 2097176
  3.0 0.0 copy-start.1
  3.0 1.2 %copy-done.1 = bf16[256,8,256]{2,1,0:T(8,128)(2,1)S(1)} copy-done((bf16[256,8,256]{2,1,0:T(8,128)(2,1)S(1)}, bf16[256,8,256]{2,1,0:T(8,128)(2,1)}, u32[]{:S(2)}) %copy-start.1) | copy-done | bytes 1048600
  4.2 0.0 copy-start.2
  4.2 0.9 %copy-done.2 = bf16[256,256]{1,0:T(8,128)(2,1)S(1)} copy-done((bf16[256,256]{1,0:T(8,128)(2,1)S(1)}, bf16[256,256]{1,0:T(8,128)(2,1)}, u32[]{:S(2)}) %copy-start.2) | copy-done | bytes 131096
  5.1 0.0 copy-start.3
  5.1 0.7 copy-done.3
  5.8 67.1 %shard_map.76 = (bf16[64,512]{1,0:T(8,128)(2,1)S(1)}, bf16[64,512]{1,0:T(8,128)(2,1)S(1)}, f32[8,128]{1,0:T(8,128)S(1)}) custom-call(bf16[4,64,256]{2,1,0:T(8,128)(2,1)S(1)} %bitcast.3, bf16[256,8,512]{2,1,0:T(8,128)(2,1)S(1)} %copy-done, bf16[256,8,256]{2,1,0:T(8,128)(2,1)S(1)} %copy-done.1, s32[16,2]{1,0:T(8,128)S(1)} %copy.8.sources, s32[2,2]{1,0:T(2,128)S(1)} %copy-done.3), custom_call_target="tpu_custom_call" | custom-call | tf_op jit(solution)/shard_map/pallas_call | solution.py:302
  72.9 0.5 slice_bitcast_fusion
  73.4 0.6 copy.11
  74.0 0.6 copy.12
Async XLA Ops:
  1.4 1.6 %copy-start = (bf16[256,8,512]{2,1,0:T(8,128)(2,1)S(1)}, bf16[256,8,512]{2,1,0:T(8,128)(2,1)}, u32[]{:S(2)}) copy-start(bf16[256,8,512]{2,1,0:T(8,128)(2,1)} %left.1) | copy-start | bytes 6291460
  3.0 1.2 %copy-start.1 = (bf16[256,8,256]{2,1,0:T(8,128)(2,1)S(1)}, bf16[256,8,256]{2,1,0:T(8,128)(2,1)}, u32[]{:S(2)}) copy-start(bf16[256,8,256]{2,1,0:T(8,128)(2,1)} %right.1) | copy-start | bytes 3145732
  4.2 0.9 %copy-start.2 = (bf16[256,256]{1,0:T(8,128)(2,1)S(1)}, bf16[256,256]{1,0:T(8,128)(2,1)}, u32[]{:S(2)}) copy-start(bf16[256,256]{1,0:T(8,128)(2,1)} %param.5) | copy-start | bytes 393220
  5.1 0.7 copy-start.3

commit v2 on v1

v2 whole, which is shorter than its diff:
```python
import functools

import jax
import jax.numpy as jnp
from jax import lax
from jax.experimental import pallas as pl
from jax.experimental.pallas import tpu as pltpu
from jax.sharding import PartitionSpec as P

EPSILON = 1e-06
MESH = pl.DeviceIdType.MESH
F32 = jnp.float32
BF16 = jnp.bfloat16


def kernel(
    B, T, R, blocks,
    wf, left, right, sources, live,
    nb_out, img_out, proj_out,
    left_raw, left_f, left_w, right_raw, right_got, right_f, right_w,
    v1, vm, v2, sbuf, half, part1, part2, red1, red2, f_ref, fb, sc_a, sc_b,
    loc_sem, rsend, rrecv, v_send, v_recv, vx_send, vx_recv, s_sem,
    p1_send, p1_recv, p2_send, p2_recv, g_send, g_recv, gx_send, gx_recv,
    sc_send, sc_recv,
):
    TR = T * R
    b, t, r = lax.axis_index("blk"), lax.axis_index("term"), lax.axis_index("rep")
    slot = t * R + r
    N = B * TR
    me = b * TR + slot
    rows, W, M = left.shape
    ro = rows // TR
    hc = M // R
    qc = M // 4
    own, u = b // 2, b % 2

    def copy(src, dst, ss, rs, bb, tt, rr):
        return pltpu.make_async_remote_copy(
            src_ref=src, dst_ref=dst, send_sem=ss, recv_sem=rs,
            device_id={"blk": bb, "term": tt, "rep": rr}, device_id_type=MESH)

    def zpeer(k):
        p, bit = b, 1
        while bit < B:
            if k & bit:
                p = p + bit - 2 * bit * (b // bit % 2)
            bit *= 2
        return p

    zfrom = zpeer

    def speer(k):
        p = lax.rem(slot + k, TR)
        return p // R, lax.rem(p, R)

    def peer(k):
        p = lax.rem(me + k, N)
        q = lax.rem(p, TR)
        return {"blk": p // TR, "term": q // R, "rep": lax.rem(q, R)}

    barrier = pltpu.get_barrier_semaphore()

    @pl.loop(1, N)
    def _(k):
        pl.semaphore_signal(barrier, inc=1, device_id=peer(k), device_id_type=MESH)

    lcopy = pltpu.make_async_copy(left, left_raw, loc_sem.at[0])
    lcopy.start()
    rcopy = pltpu.make_async_copy(right, right_raw, loc_sem.at[1])
    rcopy.start()
    wcopy = pltpu.make_async_copy(wf, v1.at[own, pl.ds(u * TR, TR)], loc_sem.at[2])
    wcopy.start()
    pl.semaphore_wait(barrier, N - 1)

    def piece(buf, bb, start, n):
        return buf.at[bb // 2, pl.ds((bb % 2) * TR + start, n)]

    vz = []
    for k in range(1, B):
        c = copy(wf.at[pl.ds(t * R, R)], piece(v1, b, t * R, R), v_send.at[k - 1], v_recv.at[k - 1], zpeer(k), t, r)
        c.start()
        vz.append(c)
    mine = [copy(wf.at[t * R + lax.rem(r + 1, R)], sbuf, s_sem.at[0], s_sem.at[1], b, t, lax.rem(r + 1, R))]
    mine[0].start()
    other = b + 1 - 2 * u
    chunk = rows // 4
    rz = []
    for c in range(4):
        d = pl.ds(c * chunk, chunk)
        cp = copy(right.at[d], right_got.at[d], rsend.at[c], rrecv.at[c], other, t, r)
        cp.start()
        rz.append(cp)

    lcopy.wait()
    left_f[...] = left_raw[...].astype(F32)
    for w in range(W):
        left_w[w] = left_f[:, w, :].astype(BF16)
    vx = []
    for k in range(1, B):
        src = zfrom(k)
        here = piece(v1, src, t * R, R)
        copy(here, here, v_send.at[k - 1], v_recv.at[k - 1], src, t, r).wait_recv()
        for j in range(1, T):
            c = copy(here, here, vx_send.at[k - 1, j - 1], vx_recv.at[k - 1, j - 1], b, lax.rem(t + j, T), r)
            c.start()
            vx.append(c)
    rcopy.wait()
    right_f[...] = right_raw[...].astype(F32)
    for w in range(W):
        right_w[u, :, w * hc:(w + 1) * hc] = right_f[:, w, :].astype(BF16)

    for k in range(1, B):
        src = zfrom(k)
        for j in range(1, T):
            tt = lax.rem(t - j + T, T)
            there = piece(v1, src, tt * R, R)
            copy(there, there, vx_send.at[k - 1, j - 1], vx_recv.at[k - 1, j - 1], b, tt, r).wait_recv()
    wcopy.wait()
    row_of = lax.broadcasted_iota(jnp.int32, (2 * TR, ro, hc), 0) * ro + lax.broadcasted_iota(jnp.int32, (2 * TR, ro, hc), 1)
    col_of = lax.broadcasted_iota(jnp.int32, (2 * TR, ro, hc), 2) + r * hc

    @pl.loop(0, blocks)
    def _(k):
        ok = (row_of < live[k, 0]) & (col_of < live[k, 1])
        vm[k] = jnp.where(ok, v1[k].astype(F32), 0.0).astype(BF16)

    def halfway(v):
        for w in range(W):
            src = sources[own, t * W + w]
            x = v[src].reshape(M, hc)
            half[:, w * hc:(w + 1) * hc] = jnp.dot(left_w[w], x, preferred_element_type=F32).astype(BF16)

    def product(h, lo, n):
        return lax.dot_general(half[...], right_w[h, lo:lo + n, :], (((1,), (1,)), ((), ())), preferred_element_type=F32)

    def scatter(part, red, sends, recvs, q, p):
        out = []
        for k in range(1, TR):
            tt, rr = speer(k)
            c = copy(part.at[q, pl.ds(lax.rem(slot + k, TR) * ro, ro)], red.at[q, k - 1],
                     sends.at[p, k - 1], recvs.at[p, k - 1], b, tt, rr)
            c.start()
            out.append(c)
        return out

    out_row = lax.broadcasted_iota(jnp.int32, (ro, M), 0) + u * rows + slot * ro
    out_col = lax.broadcasted_iota(jnp.int32, (ro, M), 1)
    out_live = (out_row < live[own, 0]) & (out_col < live[own, 1])

    def gathered(part, red):
        got = []
        for q in range(4):
            x = part[q, pl.ds(slot * ro, ro), :]
            for k in range(1, TR):
                x = x + red[q, k - 1]
            got.append(x)
        return jnp.where(out_live, jnp.concatenate(got, axis=1), 0.0)

    def await_all(copies):
        for c in copies:
            c.wait()

    halfway(vm)
    x = product(u, 0, 2 * qc)
    part1[2 * u] = x[:, :qc]
    part1[2 * u + 1] = x[:, qc:]
    p1 = scatter(part1, red1, p1_send, p1_recv, 2 * u, 0)
    p1 += scatter(part1, red1, p1_send, p1_recv, 2 * u + 1, 1)
    for c in range(4):
        rz[c].wait()
        lo = c * chunk
        right_f[lo:lo + chunk] = right_got[lo:lo + chunk].astype(F32)
        for w in range(W):
            right_w[1 - u, lo:lo + chunk, w * hc:(w + 1) * hc] = right_f[lo:lo + chunk, w, :].astype(BF16)
        if c % 2:
            q = 2 * (1 - u) + c // 2
            part1[q] = product(1 - u, c // 2 * qc, qc)
            p1 += scatter(part1, red1, p1_send, p1_recv, q, 2 + c // 2)

    mine[0].wait()
    kept = v1[own, u * TR + slot]
    for_r0 = jnp.concatenate([kept, sbuf[...]], axis=1).astype(F32)
    for_r1 = jnp.concatenate([sbuf[...], kept], axis=1).astype(F32)
    start = jnp.where(out_live, jnp.where(r == 0, for_r0, for_r1), 0.0)
    await_all(p1)
    first = gathered(part1, red1)
    f_ref[...] = first

    for j in range(R):
        fb[j] = first[:, j * hc:(j + 1) * hc].astype(BF16)
    v2[own, u * TR + slot] = fb[r]
    gz = []
    for k in range(B):
        for j in range(R):
            rr = lax.rem(r + j, R)
            if k or j:
                i = j * B + k - 1
                c = copy(fb.at[rr], v2.at[own, u * TR + slot], g_send.at[i], g_recv.at[i], zpeer(k), t, rr)
                c.start()
                gz.append(c)

    def lane_sums(x):
        y = jnp.sum(x, axis=0, keepdims=True)
        z = y[:, :128]
        for i in range(1, M // 128):
            z = z + y[:, i * 128:(i + 1) * 128]
        return z

    def shared(buf, base, k):
        return pltpu.make_async_remote_copy(
            src_ref=buf.at[me], dst_ref=buf.at[me], send_sem=sc_send.at[base, k - 1], recv_sem=sc_recv.at[base, k - 1],
            device_id=peer(k), device_id_type=MESH)

    def spread(buf, base):
        @pl.loop(1, N)
        def _(k):
            shared(buf, base, k).start()

    def collect(buf, base):
        @pl.loop(1, N)
        def _(k):
            shared(buf, base, k).wait()

        return jnp.sum(jnp.sum(buf[...], axis=0), axis=1, keepdims=True)

    sc_a[me, 0:1] = lane_sums(start * start)
    sc_a[me, 1:2] = lane_sums(start * first)
    sc_a[me, 2:3] = lane_sums(first * first)
    sc_a[me, 3:4] = jnp.zeros((1, 128), F32)
    spread(sc_a, 0)

    def onward(k, j, to):
        src = zfrom(k)
        rr = lax.rem(r - j + R, R)
        at = lax.rem(t - to + T, T)
        sent = v2.at[src // 2, (src % 2) * TR + t * R + rr]
        got = v2.at[src // 2, (src % 2) * TR + at * R + rr]
        go = copy(sent, sent, gx_send.at[k * R + j, to - 1], gx_recv.at[k * R + j, to - 1], b, lax.rem(t + to, T), r)
        came = copy(got, got, gx_send.at[k * R + j, to - 1], gx_recv.at[k * R + j, to - 1], b, at, r)
        return go, came

    for k in range(B):
        src = zfrom(k)
        for j in range(R):
            if k or j:
                i = j * B + k - 1
                rr = lax.rem(r - j + R, R)
                there = v2.at[src // 2, (src % 2) * TR + t * R + rr]
                copy(there, there, g_send.at[i], g_recv.at[i], src, t, rr).wait_recv()
            for to in range(1, T):
                onward(k, j, to)[0].start()
    for k in range(B):
        for j in range(R):
            for to in range(1, T):
                onward(k, j, to)[1].wait_recv()

    halfway(v2)
    p2 = []
    for i in range(2):
        h = u if i == 0 else 1 - u
        x = product(h, 0, 2 * qc)
        for c in range(2):
            part2[2 * h + c] = x[:, c * qc:(c + 1) * qc]
            p2 += scatter(part2, red2, p2_send, p2_recv, 2 * h + c, 2 * i + c)

    total = collect(sc_a, 0)
    self_product, cross, square = total[0:1], total[1:2], total[2:3]
    rayleigh = cross / (self_product + EPSILON)
    residual_square = jnp.maximum(square - 2.0 * rayleigh * cross + rayleigh * rayleigh * self_product, 0.0)
    entries = float(blocks * M * M)
    scale = lax.rsqrt(residual_square / entries + EPSILON)
    first = f_ref[...]
    nb = ((first - rayleigh * start) * scale).astype(BF16)
    nb_out[...] = nb

    await_all(p2)
    second = gathered(part2, red2)
    image = (second - rayleigh * f_ref[...]) * scale
    img_out[...] = image.astype(BF16)
    sc_b[me] = lane_sums(nb.astype(F32) * image)
    spread(sc_b, 1)
    correlation = collect(sc_b, 1) / entries
    lane = lax.broadcasted_iota(jnp.int32, (8, 128), 1)
    proj_out[...] = jnp.where(lane == 0, rayleigh, correlation)
    for c in vz + vx + gz:
        c.wait_send()
    for k in range(B):
        for j in range(R):
            for to in range(1, T):
                onward(k, j, to)[0].wait_send()


def finish(nb, img, proj, nb_out, img_out, proj_out):
    nb_out[...] = nb[...]
    img_out[...] = img[...]
    lane = lax.broadcasted_iota(jnp.int32, (8, 128), 1)
    row = lax.broadcasted_iota(jnp.int32, (8, 128), 0)
    for i in range(2):
        proj_out[i] = jnp.sum(jnp.where((lane == i) & (row == 0), proj[...], 0.0))


def local(wavefunction, left_env, right_env, sources, live_dims):
    B, T, R = lax.axis_size("blk"), lax.axis_size("term"), lax.axis_size("rep")
    TR = T * R
    rows, W, M = left_env.shape
    hc = M // R
    ro = rows // TR
    qc = M // 4
    blocks = live_dims.shape[0]
    vmem = pl.BlockSpec(memory_space=pltpu.VMEM)
    smem = pl.BlockSpec(memory_space=pltpu.SMEM)
    anyw = pl.BlockSpec(memory_space=pltpu.HBM)
    dma = pltpu.SemaphoreType.DMA
    V = pltpu.VMEM
    nb, img, proj = pl.pallas_call(
        functools.partial(kernel, B, T, R, blocks),
        out_shape=(
            jax.ShapeDtypeStruct((ro, M), BF16),
            jax.ShapeDtypeStruct((ro, M), BF16),
            jax.ShapeDtypeStruct((8, 128), F32),
        ),
        in_specs=[anyw, anyw, anyw, smem, smem],
        out_specs=(vmem, vmem, vmem),
        scratch_shapes=[
            V((rows, W, M), BF16), V((rows, W, M), F32), V((W, rows, M), BF16),
            V((rows, W, hc), BF16), V((rows, W, hc), BF16), V((rows, W, hc), F32),
            V((2, rows, W * hc), BF16),
            V((blocks, 2 * TR, ro, hc), BF16), V((blocks, 2 * TR, ro, hc), BF16), V((blocks, 2 * TR, ro, hc), BF16),
            V((ro, hc), BF16), V((rows, W * hc), BF16),
            V((4, rows, qc), F32), V((4, rows, qc), F32),
            V((4, TR - 1, ro, qc), F32), V((4, TR - 1, ro, qc), F32),
            V((ro, M), F32), V((R, ro, hc), BF16),
            V((B * TR, 4, 128), F32), V((B * TR, 1, 128), F32),
            dma((3,)), dma((4,)), dma((4,)), dma((B - 1,)), dma((B - 1,)), dma((B - 1, T - 1)), dma((B - 1, T - 1)), dma((2,)),
            dma((4, TR - 1)), dma((4, TR - 1)), dma((4, TR - 1)), dma((4, TR - 1)),
            dma((R * B - 1,)), dma((R * B - 1,)), dma((B * R, T - 1)), dma((B * R, T - 1)),
            dma((2, B * TR - 1)), dma((2, B * TR - 1)),
        ],
        compiler_params=pltpu.CompilerParams(collective_id=0, has_side_effects=True, vmem_limit_bytes=62 * 2**20),
    )(wavefunction.reshape(TR, ro, hc), left_env, right_env, sources.T, live_dims)
    return pl.pallas_call(
        finish,
        out_shape=(
            jax.ShapeDtypeStruct((ro, M), BF16),
            jax.ShapeDtypeStruct((ro, M), BF16),
            jax.ShapeDtypeStruct((2,), F32),
        ),
        in_specs=[vmem, vmem, vmem],
        out_specs=(vmem, vmem, smem),
    )(nb, img, proj)


def solution(mesh):
    return jax.shard_map(
        local,
        mesh=mesh,
        in_specs=(
            P(("groups", "blk"), "rep"),
            P(("groups", "blk"), "term", None),
            P(("groups", "blk"), "term", "rep"),
            P("groups", None),
            P("groups", None),
        ),
        out_specs=(
            P(("groups", "blk", "term", "rep"), None),
            P(("groups", "blk", "term", "rep"), None),
            P("groups"),
        ),
        check_vma=False,
    )
```

time: 74.9 us -> 67.2 us (0.90)
  local copies, waits for them, and re-layouts: 6.92 us -> 0 us
  Pallas kernels: 67.1 us -> 66.2 us
    unnamed x11 -> x0, local copies, waits for them, and re-layouts: 6.41 us -> none
    pallas_call x1, Pallas kernels: 67.1 us -> 64.7 us  [local(): pl.pallas_call(functools.partial(kernel, B, T, R, blocks), out_shape=(jax...]
    pallas_call x0 -> x1, Pallas kernels: none -> 1.54 us  [local(): pl.pallas_call(finish, out_shape=(jax.ShapeDtypeStruct((ro, M), BF16), ja...]
where the time goes in v2:
time: 67.2 us; the launch traced here: 67 us
  Pallas kernels  66.2 us (99%)
  between operations  0.8 us (1%)
    pallas_call x1, Pallas kernels, local(): pl.pallas_call(functools.partial(kernel, B, T, R, blocks), out_shape=(jax...  64.7 us
    pallas_call x1, Pallas kernels, local(): pl.pallas_call(finish, out_shape=(jax.ShapeDtypeStruct((ro, M), BF16), ja...  1.54 us

profile of v2, /device:TPU:0, one launch (start us, length us, event | category | flops | bytes accessed | tf_op | source)
XLA Modules:
  0.0 67.0 jit_solution(16941147461923303240)
XLA Ops:
  0.6 64.7 %shard_map.76 = (bf16[64,512]{1,0:T(8,128)(2,1)}, bf16[64,512]{1,0:T(8,128)(2,1)}, f32[8,128]{1,0:T(8,128)}) custom-call(bf16[4,64,256]{2,1,0:T(8,128)(2,1)} %bitcast.2, bf16[256,8,512]{2,1,0:T(8,128)(2,1)} %left.1, bf16[256,8,256]{2,1,0:T(8,128)(2,1)} %right.1, s32[2,16]{1,0:T(2,128)} %bitcast.3, s32[2,2]{1,0:T(2,128)} %live.1), custom_call_target="tpu_custom_call" | custom-call | tf_op jit(solution)/shard_map/pallas_call | solution.py:315
  65.3 1.5 %shard_map.77 = (bf16[64,512]{1,0:T(8,128)(2,1)}, bf16[64,512]{1,0:T(8,128)(2,1)}, f32[2]{0:T(128)}) custom-call(bf16[64,512]{1,0:T(8,128)(2,1)} %get-tuple-element.6.nb, bf16[64,512]{1,0:T(8,128)(2,1)} %get-tuple-element.7.img, f32[8,128]{1,0:T(8,128)} %get-tuple-element.8.proj), custom_call_target="tpu_custom_call" | custom-call | tf_op jit(solution)/shard_map/pallas_call | solution.py:341
